TPU v7x, 32 devices: a whole 2x2x4 slice. The times are simulated.
32 devices in a mesh: basin: 8 (over z, x), ens: 4 (over y, core).
Axes of the slice: x: 2, y: 2, z: 4, core: 2. Of those that a mesh axis runs over, the one named last changes fastest.
Arguments:
- downstream: int32 [8192], P('basin'), may hold values from 0 to 8191, as said below
- bed_level: float32 [8192], P('basin'), may hold values from 0 to 3
- reach_length: float32 [8192], P('basin'), may hold values from 1000 to 5000
- channel_width: float32 [8192], P('basin'), may hold values from 50 to 300
- roughness: float32 [8192], P('basin'), may hold values from 0.025 to 0.06
- depth: float32 [8192, 512], P('basin', 'ens'), may hold values from 0.5 to 3
- flow: float32 [8192, 512], P('basin', 'ens'), may hold values from 0 to 2
- runoff: float32 [8192, 512], P('basin', 'ens'), may hold values from 0.0002 to 0.005
Outputs:
- new_depth: float32 [8192, 512], P('basin', 'ens')
- new_flow: float32 [8192, 512], P('basin', 'ens')
- mean_flow: float32 [8192], P('basin')
Inputs may be any that keep to these rules, and one draw needn't show every extreme that they name: `downstream`: within the 1024 cells of one block, a cell drains either into a later cell of the same block, into itself (mouth), or into a cell of the next block or of the block after it along basin (main-stem segments); from one block at most 256 cells drain into each of these two, and exactly 256 into the next one wherever it exists.
All inputs are finite; a program needn't handle non-finite values.
Results may differ from a plain program's by a relative error of at most 0.0001.
Values sent between devices are 32-bit elements; how exact they have to be, the bound alone decides.
A program may use at most 64 MiB of HBM per device.

v0:
```python
import functools

import jax
import jax.numpy as jnp
from jax import lax
from jax.experimental import pallas as pl
from jax.experimental.pallas import tpu as pltpu
from jax.sharding import PartitionSpec as P

SLOTS = 256
STEPS = 4
GRAVITY = 9.81
TIME_STEP = 30.0
DEPTH_FLOOR = 0.25

BF16 = jnp.bfloat16
F32 = jnp.float32
MESH = pl.DeviceIdType.MESH

T_LOCAL, T_REMOTE, BED, BED_DOWN, SLOPE_K, CAP, WIDTH, FRICTION, INV_AREA = range(9)
M_HEAD, M_TABLE, M_FLOW, M_DOWN, M_UP = 0, 2, 4, 6, 6 + 2 * STEPS
M_SUM = 6 + 4 * STEPS


def dot(a, b):
    return jnp.dot(a, b, preferred_element_type=F32)


def dot_nt(a, b):
    return lax.dot_general(a, b, (((1,), (1,)), ((), ())), preferred_element_type=F32)


def pieces(x):
    high = x.astype(BF16)
    rest = x - high.astype(F32)
    middle = rest.astype(BF16)
    low = (rest - middle.astype(F32)).astype(BF16)
    return jnp.concatenate([high, middle, low], axis=0)


def halves(x):
    high = x.astype(BF16)
    return high, (x - high.astype(F32)).astype(BF16)


def kernel(
    n_basin, n_ens, ds_ref, bed_ref, len_ref, wid_ref, rough_ref, depth_ref, flow_ref, runoff_ref,
    new_depth, new_flow, mean_out,
    head, head_in, table, table_in, perm, unperm, tmap, emap, smap, par, h_buf, q_buf, r_buf,
    split_a, split_b, split_c, hd_buf, up_out, up_in, down_in, acc, edge_split, sums, sums_in,
    send_sem, recv_sem,
):
    count = depth_ref.shape[0]
    members = depth_ref.shape[1]
    tiles = count // 128
    p = lax.axis_index("basin")
    e = lax.axis_index("ens")

    def dn(index, hop, src, dst):
        return pltpu.make_async_remote_copy(
            src_ref=src, dst_ref=dst, send_sem=send_sem.at[index + hop],
            recv_sem=recv_sem.at[index + hop],
            device_id={"basin": lax.rem(p + hop + 1, n_basin)}, device_id_type=MESH,
        )

    def up(index, hop, src, dst):
        return pltpu.make_async_remote_copy(
            src_ref=src, dst_ref=dst, send_sem=send_sem.at[index + hop],
            recv_sem=recv_sem.at[index + hop],
            device_id={"basin": lax.rem(p + n_basin - hop - 1, n_basin)}, device_id_type=MESH,
        )

    def has_lower(hop):
        return p + (hop + 1) < n_basin

    def has_upper(hop):
        return p >= hop + 1

    barrier = pltpu.get_barrier_semaphore()
    for hop in range(2):
        @pl.when(has_lower(hop))
        def _(hop=hop):
            pl.semaphore_signal(barrier, inc=1, device_id={"basin": p + hop + 1}, device_id_type=MESH)

        @pl.when(has_upper(hop))
        def _(hop=hop):
            pl.semaphore_signal(barrier, inc=1, device_id={"basin": p - hop - 1}, device_id_type=MESH)
    for d in range(1, n_ens):
        pl.semaphore_signal(barrier, inc=1, device_id={"ens": lax.rem(e + d, n_ens)}, device_id_type=MESH)

    rel = ds_ref[...] - p * count
    own = lax.broadcasted_iota(jnp.int32, (tiles, 128), 0) * 128 + lax.broadcasted_iota(
        jnp.int32, (tiles, 128), 1
    )
    near = (rel >= count) & (rel < 2 * count)
    far = rel >= 2 * count
    mouth = rel == own
    target = rel - jnp.where(near, count, 0) - jnp.where(far, 2 * count, 0)
    kind = jnp.where(near, 1.0, jnp.where(far, 2.0, jnp.where(mouth, 3.0, 0.0)))
    before = (
        lax.broadcasted_iota(jnp.int32, (128, 128), 0) < lax.broadcasted_iota(jnp.int32, (128, 128), 1)
    ).astype(BF16)
    ones = jnp.ones((128, 128), BF16)

    def ranks(mask):
        m = mask.astype(F32).astype(BF16)
        within = dot(m, before)
        totals = dot(m, ones)
        offsets, total = [], jnp.zeros((1, 128), F32)
        for t in range(tiles):
            offsets.append(total)
            total = total + totals[t:t + 1]
        return within + jnp.concatenate(offsets, axis=0), total

    rank1, n1 = ranks(near)
    rank2, n2 = ranks(far)
    rank0, _ = ranks(jnp.logical_not(near | far))
    gap1 = SLOTS - n1
    gap2 = SLOTS - n2
    place0 = jnp.where(
        rank0 < gap1, n1 + rank0,
        jnp.where(rank0 < gap1 + gap2, SLOTS + n2 + (rank0 - gap1), n1 + n2 + rank0),
    )
    place = jnp.where(near, rank1, jnp.where(far, SLOTS + rank2, place0))

    def to_row(ref, row, value):
        for t in range(tiles):
            ref[row:row + 1, t * 128:(t + 1) * 128] = value[t:t + 1]

    length = len_ref[...]
    width = wid_ref[...]
    rough = rough_ref[...]
    to_row(head, 0, place)
    to_row(head, 1, bed_ref[...])
    to_row(head, 2, target.astype(F32))
    to_row(head, 3, kind)
    head[4:8] = jnp.zeros((4, count), F32)
    to_row(table, SLOPE_K, (GRAVITY * TIME_STEP) / length)
    to_row(table, CAP, length / (2.0 * TIME_STEP))
    to_row(table, WIDTH, width)
    to_row(table, FRICTION, GRAVITY * TIME_STEP * rough * rough)
    to_row(table, INV_AREA, TIME_STEP / (width * length))

    peers = n_ens - 1
    for hop in range(2):
        peers = peers + lax.div(p + (n_basin - hop - 1), n_basin)
        peers = peers + lax.div(2 * n_basin - p - hop - 2, n_basin)
    pl.semaphore_wait(barrier, peers)

    for hop in range(2):
        @pl.when(has_upper(hop))
        def _(hop=hop):
            up(M_HEAD, hop, head, head_in.at[hop]).start()

    for hop in range(2):
        @pl.when(jnp.logical_not(has_upper(hop)))
        def _(hop=hop):
            rows = lax.broadcasted_iota(jnp.int32, (8, SLOTS), 0)
            table_in[hop] = jnp.where(rows == T_REMOTE, -1.0, 1.0)
            q_buf[count + hop * SLOTS:count + (hop + 1) * SLOTS] = jnp.zeros((SLOTS, members), F32)
            for step in range(STEPS):
                down_in[step, hop] = jnp.zeros((SLOTS, members), F32)

        @pl.when(jnp.logical_not(has_lower(hop)))
        def _(hop=hop):
            head_in[hop] = jnp.zeros((8, count), F32)
            for step in range(STEPS):
                up_in[step, hop] = jnp.zeros((SLOTS, members), F32)

    def one_hot_rows(ref, index_row, base, columns):
        def body(t, carry):
            rows = pl.ds(pl.multiple_of(t * 64, 64), 64)
            at = (lax.broadcasted_iota(jnp.int32, (64, columns), 0) + t * 64).astype(F32)
            ref[rows, base:base + columns] = jnp.where(at == index_row, 1.0, 0.0).astype(BF16)
            return carry
        lax.fori_loop(0, count // 64, body, 0)

    one_hot_rows(perm, head[0:1, :], 0, count)

    def split_into(dst, src):
        def body(t, carry):
            rows = pl.ds(pl.multiple_of(t * 128, 128), 128)
            high, low = halves(src[rows, :])
            dst[rows, :members] = high
            dst[rows, members:] = low
            return carry
        lax.fori_loop(0, count // 128, body, 0)

    split_into(split_a, depth_ref)
    split_into(split_b, flow_ref)
    split_into(split_c, runoff_ref)

    def joined(a, b):
        out = dot(a, b)
        return out[:, :members] + out[:, members:]

    def chunk(c, size=SLOTS):
        return slice(c * size, (c + 1) * size)

    for c in range(count // SLOTS):
        h_buf[0, chunk(c)] = joined(perm[chunk(c)], split_a[...])
        q_buf[chunk(c)] = joined(perm[chunk(c)], split_b[...])
        if c < 2:
            @pl.when(has_lower(c))
            def _(c=c):
                dn(M_FLOW, c, q_buf.at[pl.ds(c * SLOTS, SLOTS)], q_buf.at[pl.ds(count + c * SLOTS, SLOTS)]).start()
                dn(M_DOWN, c, h_buf.at[0, pl.ds(c * SLOTS, SLOTS)], down_in.at[0, c]).start()

    one_hot_rows(tmap, head[2:3, :], 0, count)
    for hop in range(2):
        @pl.when(has_lower(hop))
        def _(hop=hop):
            up(M_HEAD, hop, head, head_in.at[hop]).wait_recv()
    looked = jnp.concatenate([head[...], head_in[0], head_in[1], jnp.zeros((8, count), F32)], axis=0)
    found3 = dot(pieces(looked), tmap[...])
    found = found3[0:32] + found3[32:64] + found3[64:96]
    kinds = head[3:4, :]
    bed_row = head[1:2, :]
    is_remote = (kinds == 1.0) | (kinds == 2.0)
    spot = jnp.where(kinds == 1.0, found[8:9], jnp.where(kinds == 2.0, found[16:17], found[0:1]))
    bed_far = jnp.where(kinds == 1.0, found[9:10], jnp.where(kinds == 2.0, found[17:18], found[1:2]))
    table[T_LOCAL:T_LOCAL + 1] = jnp.where(kinds == 0.0, spot, -1.0)
    table[T_REMOTE:T_REMOTE + 1] = jnp.where(is_remote, spot, -1.0)
    table[BED:BED + 1] = bed_row
    table[BED_DOWN:BED_DOWN + 1] = jnp.where(kinds == 3.0, bed_row - 1.0, bed_far)
    table[9:16] = jnp.zeros((7, count), F32)

    split_table = pieces(table[...])
    rows3 = dot_nt(split_table, perm[...])
    table[...] = rows3[0:16] + rows3[16:32] + rows3[32:48]
    for hop in range(2):
        @pl.when(has_lower(hop))
        def _(hop=hop):
            dn(M_TABLE, hop, table.at[pl.ds(0, 8), pl.ds(hop * SLOTS, SLOTS)], table_in.at[hop]).start()

    lanes = lax.broadcasted_iota(jnp.int32, (128, count), 1).astype(F32)

    def spread(columns, base, size, target_column, last):
        for k in range(BED, last):
            par[k - BED, base:base + size] = jnp.broadcast_to(columns[:, k:k + 1], (size, members))
        for t in range(size // 128):
            emap[base + t * 128:base + (t + 1) * 128] = jnp.where(
                columns[t * 128:(t + 1) * 128, target_column:target_column + 1] == lanes, 1.0, 0.0
            ).astype(BF16)

    for c in range(count // SLOTS):
        cols3 = dot_nt(perm[chunk(c)], split_table)
        spread(cols3[:, 0:16] + cols3[:, 16:32] + cols3[:, 32:48], c * SLOTS, SLOTS, T_LOCAL, 9)
    one_hot_rows(smap, table[T_LOCAL:T_LOCAL + 1], 0, count)

    eye = (
        lax.broadcasted_iota(jnp.int32, (SLOTS, SLOTS), 0) == lax.broadcasted_iota(jnp.int32, (SLOTS, SLOTS), 1)
    ).astype(BF16)
    blank = jnp.zeros((8, SLOTS), F32)
    for hop in range(2):
        @pl.when(has_upper(hop))
        def _(hop=hop):
            dn(M_TABLE, hop, table.at[pl.ds(0, 8), pl.ds(hop * SLOTS, SLOTS)], table_in.at[hop]).wait_recv()
        cols3 = dot_nt(eye, pieces(jnp.concatenate([table_in[hop], blank], axis=0)))
        spread(cols3[:, 0:16] + cols3[:, 16:32] + cols3[:, 32:48], count + hop * SLOTS, SLOTS, T_REMOTE, 8)

    def send_up(step):
        for hop in range(2):
            up_out[step, hop] = joined(emap[count + hop * SLOTS:count + (hop + 1) * SLOTS], split_a[...])

            @pl.when(has_upper(hop))
            def _(hop=hop):
                up(M_UP + 2 * step, hop, up_out.at[step, hop], up_in.at[step, hop]).start()

    split_into(split_a, h_buf.at[0])
    send_up(0)
    for hop in range(2):
        one_hot_rows(smap, table_in[hop, T_REMOTE:T_REMOTE + 1], count + hop * SLOTS, SLOTS)
    for c in range(count // SLOTS):
        r_buf[chunk(c)] = joined(perm[chunk(c)], split_c[...]) * TIME_STEP

    eye8 = eye[:128, :128]
    place_t = dot_nt(eye8, pieces(jnp.concatenate([place, jnp.zeros((16 - tiles, 128), F32)], axis=0)))
    place_t = place_t[:, 0:16] + place_t[:, 16:32] + place_t[:, 32:48]
    for t in range(tiles):
        unperm[t * 128:(t + 1) * 128] = jnp.where(place_t[:, t:t + 1] == lanes, 1.0, 0.0).astype(BF16)

    def momentum(rows, q, h, hd):
        bed = par[0, rows, :]
        bed_down = par[1, rows, :]
        level = bed + h
        level_down = bed_down + hd
        deep = jnp.maximum(jnp.maximum(level, level_down) - jnp.maximum(bed, bed_down), DEPTH_FLOOR)
        root = jnp.exp2(jnp.log2(deep) * (-7.0 / 3.0))
        moved = (q - deep * (level_down - level) * par[2, rows, :]) / (
            1.0 + par[5, rows, :] * jnp.abs(q) * root
        )
        q = jnp.minimum(moved, h * par[3, rows, :])
        q_buf[rows, :] = q
        high, low = halves(q * par[4, rows, :])
        edge_split[rows, :members] = high
        edge_split[rows, members:] = low

    block = 64
    for step in range(STEPS):
        last = step == STEPS - 1
        for c in range(count // SLOTS):
            hd_buf[chunk(c)] = joined(emap[chunk(c)], split_a[...])

        def inner(t, carry):
            rows = pl.ds(pl.multiple_of(2 * SLOTS + t * block, block), block)
            momentum(rows, q_buf[rows, :], h_buf[step, rows, :], hd_buf[rows, :])
            return carry
        if step == 0:
            for hop in range(2):
                @pl.when(has_lower(hop))
                def _(hop=hop):
                    dn(M_FLOW, hop, q_buf.at[pl.ds(hop * SLOTS, SLOTS)], q_buf.at[pl.ds(count + hop * SLOTS, SLOTS)]).wait_send()
        lax.fori_loop(0, (count - 2 * SLOTS) // block, inner, 0)
        for c in range(count // SLOTS):
            acc[chunk(c)] = joined(smap[chunk(c), 2 * SLOTS:count], edge_split[2 * SLOTS:count])
        for hop in range(2):
            @pl.when(has_lower(hop))
            def _(hop=hop):
                up(M_UP + 2 * step, hop, up_out.at[step, hop], up_in.at[step, hop]).wait_recv()

            def outer(t, carry):
                at = pl.ds(pl.multiple_of(t * block, block), block)
                rows = pl.ds(pl.multiple_of(hop * SLOTS + t * block, block), block)
                momentum(rows, q_buf[rows, :], h_buf[step, rows, :], hd_buf[rows, :] + up_in[step, hop, at, :])
                return carry
            lax.fori_loop(0, SLOTS // block, outer, 0)

        if last:
            for t in range(count // 128):
                rows = slice(t * 128, (t + 1) * 128)
                high, low = halves(q_buf[rows])
                split_b[rows, :members] = high
                split_b[rows, members:] = low
            for c in range(count // SLOTS):
                new_flow[chunk(c)] = joined(unperm[chunk(c)], split_b[...])
            one = jnp.ones((16, members), BF16)
            high, low = halves(new_flow[...])
            sums[...] = (dot_nt(one, high) + dot_nt(one, low))[0:8]
            for d in range(1, n_ens):
                pltpu.make_async_remote_copy(
                    src_ref=sums, dst_ref=sums_in.at[d - 1], send_sem=send_sem.at[M_SUM + d - 1],
                    recv_sem=recv_sem.at[M_SUM + d - 1],
                    device_id={"ens": lax.rem(e + d, n_ens)}, device_id_type=MESH,
                ).start()

        for hop in range(2):
            @pl.when(has_upper(hop))
            def _(hop=hop):
                if step == 0:
                    dn(M_FLOW, hop, q_buf.at[pl.ds(hop * SLOTS, SLOTS)], q_buf.at[pl.ds(count + hop * SLOTS, SLOTS)]).wait_recv()
                dn(M_DOWN + 2 * step, hop, h_buf.at[step, pl.ds(hop * SLOTS, SLOTS)], down_in.at[step, hop]).wait_recv()

            def ghost(t, carry):
                at = pl.ds(pl.multiple_of(t * block, block), block)
                rows = pl.ds(pl.multiple_of(count + hop * SLOTS + t * block, block), block)
                momentum(rows, q_buf[rows, :], down_in[step, hop, at, :], up_out[step, hop, at, :])
                return carry
            lax.fori_loop(0, SLOTS // block, ghost, 0)

        for c in range(count // SLOTS):
            arriving = (
                acc[chunk(c)]
                + joined(smap[chunk(c), 0:2 * SLOTS], edge_split[0:2 * SLOTS])
                + joined(smap[chunk(c), count:], edge_split[count:])
            )
            fresh = h_buf[step, chunk(c)] + (
                r_buf[chunk(c)] + (arriving - q_buf[chunk(c)] * par[4, chunk(c)]) * par[6, chunk(c)]
            )
            h_buf[step + 1, chunk(c)] = fresh
            if c < 2 and not last:
                @pl.when(has_lower(c))
                def _(c=c):
                    dn(M_DOWN + 2 * step + 2, c, h_buf.at[step + 1, pl.ds(c * SLOTS, SLOTS)], down_in.at[step + 1, c]).start()
            high, low = halves(fresh)
            split_a[chunk(c), :members] = high
            split_a[chunk(c), members:] = low
        if not last:
            send_up(step + 1)

    for c in range(count // SLOTS):
        new_depth[chunk(c)] = joined(unperm[chunk(c)], split_a[...])

    total = sums[...]
    for d in range(1, n_ens):
        copy = pltpu.make_async_remote_copy(
            src_ref=sums, dst_ref=sums_in.at[d - 1], send_sem=send_sem.at[M_SUM + d - 1],
            recv_sem=recv_sem.at[M_SUM + d - 1],
            device_id={"ens": lax.rem(e + d, n_ens)}, device_id_type=MESH,
        )
        copy.wait()
        total = total + sums_in[d - 1]
    mean_out[...] = total * (1.0 / (n_ens * members))

    for hop in range(2):
        @pl.when(has_lower(hop))
        def _(hop=hop):
            dn(M_TABLE, hop, table.at[pl.ds(0, 8), pl.ds(hop * SLOTS, SLOTS)], table_in.at[hop]).wait_send()
            for step in range(STEPS):
                dn(M_DOWN + 2 * step, hop, h_buf.at[step, pl.ds(hop * SLOTS, SLOTS)], down_in.at[step, hop]).wait_send()

        @pl.when(has_upper(hop))
        def _(hop=hop):
            up(M_HEAD, hop, head, head_in.at[hop]).wait_send()
            for step in range(STEPS):
                up(M_UP + 2 * step, hop, up_out.at[step, hop], up_in.at[step, hop]).wait_send()


def per_device(downstream, bed_level, reach_length, channel_width, roughness, depth, flow, runoff):
    n_basin = lax.axis_size("basin")
    n_ens = lax.axis_size("ens")
    count, members = depth.shape
    edges = count + 2 * SLOTS
    messages = M_SUM + n_ens - 1
    tile = lambda x: x.reshape(count // 128, 128)
    whole = pl.BlockSpec(memory_space=pltpu.VMEM)
    new_depth, new_flow, mean = pl.pallas_call(
        functools.partial(kernel, n_basin, n_ens),
        out_shape=(
            jax.ShapeDtypeStruct((count, members), F32),
            jax.ShapeDtypeStruct((count, members), F32),
            jax.ShapeDtypeStruct((8, count), F32),
        ),
        in_specs=[whole] * 8,
        out_specs=(whole,) * 3,
        scratch_shapes=[
            pltpu.VMEM((8, count), F32),
            pltpu.VMEM((2, 8, count), F32),
            pltpu.VMEM((16, count), F32),
            pltpu.VMEM((2, 8, SLOTS), F32),
            pltpu.VMEM((count, count), BF16),
            pltpu.VMEM((count, count), BF16),
            pltpu.VMEM((count, count), BF16),
            pltpu.VMEM((edges, count), BF16),
            pltpu.VMEM((count, edges), BF16),
            pltpu.VMEM((7, edges, members), F32),
            pltpu.VMEM((STEPS + 1, count, members), F32),
            pltpu.VMEM((edges, members), F32),
            pltpu.VMEM((count, members), F32),
            pltpu.VMEM((count, 2 * members), BF16),
            pltpu.VMEM((count, 2 * members), BF16),
            pltpu.VMEM((count, 2 * members), BF16),
            pltpu.VMEM((count, members), F32),
            pltpu.VMEM((STEPS, 2, SLOTS, members), F32),
            pltpu.VMEM((STEPS, 2, SLOTS, members), F32),
            pltpu.VMEM((STEPS, 2, SLOTS, members), F32),
            pltpu.VMEM((count, members), F32),
            pltpu.VMEM((edges, 2 * members), BF16),
            pltpu.VMEM((8, count), F32),
            pltpu.VMEM((n_ens - 1, 8, count), F32),
            pltpu.SemaphoreType.DMA((messages,)),
            pltpu.SemaphoreType.DMA((messages,)),
        ],
        compiler_params=pltpu.CompilerParams(
            collective_id=0, has_side_effects=True, vmem_limit_bytes=56 * 1024 * 1024
        ),
    )(tile(downstream), tile(bed_level), tile(reach_length), tile(channel_width), tile(roughness), depth, flow, runoff)
    return new_depth, new_flow, mean[0]


def solution(mesh):
    cells, both = P("basin"), P("basin", "ens")
    return jax.shard_map(
        per_device,
        mesh=mesh,
        in_specs=(cells,) * 5 + (both,) * 3,
        out_specs=(both, both, cells),
        check_vma=False,
    )
```

profile of v0, /device:TPU:0, one launch (start us, length us, event | category | flops | bytes accessed | tf_op | source)
XLA Modules:
  0.0 60.4 jit_solution(12106246583813404946)
XLA Ops:
  0.6 55.7 %shard_map.103 = (f32[1024,128]{1,0:T(8,128)}, f32[1024,128]{1,0:T(8,128)}, f32[8,1024]{1,0:T(8,128)}) custom-call(s32[8,128]{1,0:T(8,128)} %bitcast.6, f32[8,128]{1,0:T(8,128)} %bitcast.7, f32[8,128]{1,0:T(8,128)} %bitcast.8, f32[8,128]{1,0:T(8,128)} %bitcast.9, f32[8,128]{1,0:T(8,128)} %bitcast.10, f32[1024,128]{1,0:T(8,128)} %depth_ref.1, ...), custom_call_target="tpu_custom_call" | custom-call | tf_op jit(solution)/shard_map/pallas_call | solution.py:417
  56.4 1.4 %slice.3 = f32[1,1024]{1,0:T(1,128)} slice(f32[8,1024]{1,0:T(8,128)} %get-tuple-element.8), slice={[0:1], [0:1024]} | slice | bytes 8192 | tf_op jit(solution)/shard_map/slice | solution.py:458
  57.7 0.0 copy-start
  57.7 1.9 %copy.13 = f32[1024,128]{1,0:T(8,128)} copy(f32[1024,128]{1,0:T(8,128)} %get-tuple-element.12) | data formatting | bytes 1048576
  59.6 0.0 copy-done
  59.6 0.8 %copy.14 = f32[1024,128]{1,0:T(8,128)} copy(f32[1024,128]{1,0:T(8,128)S(1)} %copy-done) | data formatting | bytes 1048576
Async XLA Ops:
  57.7 1.9 %copy-start = (f32[1024,128]{1,0:T(8,128)S(1)}, f32[1024,128]{1,0:T(8,128)}, u32[]{:S(2)}) copy-start(f32[1024,128]{1,0:T(8,128)} %get-tuple-element.13) | copy-start | bytes 1572868
where the time goes:
time: 60.7 us; the launch traced here: 60.4 us
  Pallas kernels  55.7 us (92%)
  local copies, waits for them, and re-layouts  4.08 us (7%)
  between operations  0.64 us (1%)
    pallas_call x1, Pallas kernels, per_device(): pl.pallas_call(functools.partial(kernel, n_basin, n_ens), out_shape=(jax....  55.7 us
    unnamed x4, local copies, waits for them, and re-layouts  2.72 us
    slice x1, local copies, waits for them, and re-layouts, per_device(): return (new_depth, new_flow, mean[0])  1.35 us

commit v1 on v0

--- a/solution.py
+++ b/solution.py
@@ -45,8 +45,8 @@
 
 def kernel(
     n_basin, n_ens, ds_ref, bed_ref, len_ref, wid_ref, rough_ref, depth_ref, flow_ref, runoff_ref,
-    new_depth, new_flow, mean_out,
-    head, head_in, table, table_in, perm, unperm, tmap, emap, smap, par, h_buf, q_buf, r_buf,
+    new_depth, new_flow, mean_out, place_out,
+    head, head_in, table, table_in, perm, tmap, emap, smap, par, h_buf, q_buf, r_buf,
     split_a, split_b, split_c, hd_buf, up_out, up_in, down_in, acc, edge_split, sums, sums_in,
     send_sem, recv_sem,
 ):
@@ -200,11 +200,6 @@
     for c in range(count // SLOTS):
         h_buf[0, chunk(c)] = joined(perm[chunk(c)], split_a[...])
         q_buf[chunk(c)] = joined(perm[chunk(c)], split_b[...])
-        if c < 2:
-            @pl.when(has_lower(c))
-            def _(c=c):
-                dn(M_FLOW, c, q_buf.at[pl.ds(c * SLOTS, SLOTS)], q_buf.at[pl.ds(count + c * SLOTS, SLOTS)]).start()
-                dn(M_DOWN, c, h_buf.at[0, pl.ds(c * SLOTS, SLOTS)], down_in.at[0, c]).start()
 
     one_hot_rows(tmap, head[2:3, :], 0, count)
     for hop in range(2):
@@ -232,6 +227,11 @@
         @pl.when(has_lower(hop))
         def _(hop=hop):
             dn(M_TABLE, hop, table.at[pl.ds(0, 8), pl.ds(hop * SLOTS, SLOTS)], table_in.at[hop]).start()
+    for hop in range(2):
+        @pl.when(has_lower(hop))
+        def _(hop=hop):
+            dn(M_DOWN, hop, h_buf.at[0, pl.ds(hop * SLOTS, SLOTS)], down_in.at[0, hop]).start()
+            dn(M_FLOW, hop, q_buf.at[pl.ds(hop * SLOTS, SLOTS)], q_buf.at[pl.ds(count + hop * SLOTS, SLOTS)]).start()
 
     lanes = lax.broadcasted_iota(jnp.int32, (128, count), 1).astype(F32)
 
@@ -273,12 +273,6 @@
         one_hot_rows(smap, table_in[hop, T_REMOTE:T_REMOTE + 1], count + hop * SLOTS, SLOTS)
     for c in range(count // SLOTS):
         r_buf[chunk(c)] = joined(perm[chunk(c)], split_c[...]) * TIME_STEP
-
-    eye8 = eye[:128, :128]
-    place_t = dot_nt(eye8, pieces(jnp.concatenate([place, jnp.zeros((16 - tiles, 128), F32)], axis=0)))
-    place_t = place_t[:, 0:16] + place_t[:, 16:32] + place_t[:, 32:48]
-    for t in range(tiles):
-        unperm[t * 128:(t + 1) * 128] = jnp.where(place_t[:, t:t + 1] == lanes, 1.0, 0.0).astype(BF16)
 
     def momentum(rows, q, h, hd):
         bed = par[0, rows, :]
@@ -296,7 +290,7 @@
         edge_split[rows, :members] = high
         edge_split[rows, members:] = low
 
-    block = 64
+    block = 128
     for step in range(STEPS):
         last = step == STEPS - 1
         for c in range(count // SLOTS):
@@ -327,16 +321,12 @@
             lax.fori_loop(0, SLOTS // block, outer, 0)
 
         if last:
-            for t in range(count // 128):
-                rows = slice(t * 128, (t + 1) * 128)
-                high, low = halves(q_buf[rows])
-                split_b[rows, :members] = high
-                split_b[rows, members:] = low
+            one = jnp.ones((16, members), BF16)
             for c in range(count // SLOTS):
-                new_flow[chunk(c)] = joined(unperm[chunk(c)], split_b[...])
-            one = jnp.ones((16, members), BF16)
-            high, low = halves(new_flow[...])
-            sums[...] = (dot_nt(one, high) + dot_nt(one, low))[0:8]
+                now = q_buf[chunk(c)]
+                new_flow[chunk(c)] = now
+                high, low = halves(now)
+                sums[:, chunk(c)] = (dot_nt(one, high) + dot_nt(one, low))[0:8]
             for d in range(1, n_ens):
                 pltpu.make_async_remote_copy(
                     src_ref=sums, dst_ref=sums_in.at[d - 1], send_sem=send_sem.at[M_SUM + d - 1],
@@ -367,8 +357,11 @@
             fresh = h_buf[step, chunk(c)] + (
                 r_buf[chunk(c)] + (arriving - q_buf[chunk(c)] * par[4, chunk(c)]) * par[6, chunk(c)]
             )
+            if last:
+                new_depth[chunk(c)] = fresh
+                continue
             h_buf[step + 1, chunk(c)] = fresh
-            if c < 2 and not last:
+            if c < 2:
                 @pl.when(has_lower(c))
                 def _(c=c):
                     dn(M_DOWN + 2 * step + 2, c, h_buf.at[step + 1, pl.ds(c * SLOTS, SLOTS)], down_in.at[step + 1, c]).start()
@@ -377,9 +370,6 @@
             split_a[chunk(c), members:] = low
         if not last:
             send_up(step + 1)
-
-    for c in range(count // SLOTS):
-        new_depth[chunk(c)] = joined(unperm[chunk(c)], split_a[...])
 
     total = sums[...]
     for d in range(1, n_ens):
@@ -391,6 +381,7 @@
         copy.wait()
         total = total + sums_in[d - 1]
     mean_out[...] = total * (1.0 / (n_ens * members))
+    place_out[...] = place
 
     for hop in range(2):
         @pl.when(has_lower(hop))
@@ -404,6 +395,33 @@
             up(M_HEAD, hop, head, head_in.at[hop]).wait_send()
             for step in range(STEPS):
                 up(M_UP + 2 * step, hop, up_out.at[step, hop], up_in.at[step, hop]).wait_send()
+
+
+def own_order(depth_ref, flow_ref, mean_ref, place_ref, new_depth, new_flow, mean_out, split):
+    count, members = depth_ref.shape
+    tiles = count // 128
+    for t in range(tiles):
+        rows = slice(t * 128, (t + 1) * 128)
+        for k, ref in enumerate((depth_ref, flow_ref)):
+            high, low = halves(ref[rows])
+            split[rows, 2 * k * members:(2 * k + 1) * members] = high
+            split[rows, (2 * k + 1) * members:(2 * k + 2) * members] = low
+    eye = (
+        lax.broadcasted_iota(jnp.int32, (128, 128), 0) == lax.broadcasted_iota(jnp.int32, (128, 128), 1)
+    ).astype(BF16)
+    place = jnp.concatenate([place_ref[...], jnp.zeros((16 - tiles, 128), F32)], axis=0)
+    place_t = dot_nt(eye, pieces(place))
+    place_t = place_t[:, 0:16] + place_t[:, 16:32] + place_t[:, 32:48]
+    lanes = lax.broadcasted_iota(jnp.int32, (128, count), 1).astype(F32)
+    mean = pieces(jnp.concatenate([mean_ref[...], mean_ref[...]], axis=0))
+    for t in range(tiles):
+        rows = slice(t * 128, (t + 1) * 128)
+        back = jnp.where(place_t[:, t:t + 1] == lanes, 1.0, 0.0).astype(BF16)
+        out = dot(back, split[...])
+        new_depth[rows] = out[:, :members] + out[:, members:2 * members]
+        new_flow[rows] = out[:, 2 * members:3 * members] + out[:, 3 * members:]
+        row = dot_nt(mean, back)
+        mean_out[t:t + 1] = row[0:1] + row[16:17] + row[32:33]
 
 
 def per_device(downstream, bed_level, reach_length, channel_width, roughness, depth, flow, runoff):
@@ -414,15 +432,16 @@
     messages = M_SUM + n_ens - 1
     tile = lambda x: x.reshape(count // 128, 128)
     whole = pl.BlockSpec(memory_space=pltpu.VMEM)
-    new_depth, new_flow, mean = pl.pallas_call(
+    moved = pl.pallas_call(
         functools.partial(kernel, n_basin, n_ens),
         out_shape=(
             jax.ShapeDtypeStruct((count, members), F32),
             jax.ShapeDtypeStruct((count, members), F32),
             jax.ShapeDtypeStruct((8, count), F32),
+            jax.ShapeDtypeStruct((count // 128, 128), F32),
         ),
         in_specs=[whole] * 8,
-        out_specs=(whole,) * 3,
+        out_specs=(whole,) * 4,
         scratch_shapes=[
             pltpu.VMEM((8, count), F32),
             pltpu.VMEM((2, 8, count), F32),
@@ -430,11 +449,10 @@
             pltpu.VMEM((2, 8, SLOTS), F32),
             pltpu.VMEM((count, count), BF16),
             pltpu.VMEM((count, count), BF16),
-            pltpu.VMEM((count, count), BF16),
             pltpu.VMEM((edges, count), BF16),
             pltpu.VMEM((count, edges), BF16),
             pltpu.VMEM((7, edges, members), F32),
-            pltpu.VMEM((STEPS + 1, count, members), F32),
+            pltpu.VMEM((STEPS, count, members), F32),
             pltpu.VMEM((edges, members), F32),
             pltpu.VMEM((count, members), F32),
             pltpu.VMEM((count, 2 * members), BF16),
@@ -455,7 +473,19 @@
             collective_id=0, has_side_effects=True, vmem_limit_bytes=56 * 1024 * 1024
         ),
     )(tile(downstream), tile(bed_level), tile(reach_length), tile(channel_width), tile(roughness), depth, flow, runoff)
-    return new_depth, new_flow, mean[0]
+    new_depth, new_flow, mean = pl.pallas_call(
+        own_order,
+        out_shape=(
+            jax.ShapeDtypeStruct((count, members), F32),
+            jax.ShapeDtypeStruct((count, members), F32),
+            jax.ShapeDtypeStruct((count // 128, 128), F32),
+        ),
+        in_specs=[whole] * 4,
+        out_specs=(whole,) * 3,
+        scratch_shapes=[pltpu.VMEM((count, 4 * members), BF16)],
+        compiler_params=pltpu.CompilerParams(vmem_limit_bytes=56 * 1024 * 1024),
+    )(*moved)
+    return new_depth, new_flow, mean.reshape(count)
 
 
 def solution(mesh):

time: 60.7 us -> 54.5 us (0.90)
  local copies, waits for them, and re-layouts: 4.08 us -> 0 us
  Pallas kernels: 55.7 us -> 53.7 us
    pallas_call x1, Pallas kernels: 55.7 us -> 49.6 us  [per_device(): pl.pallas_call(functools.partial(kernel, n_basin, n_ens), out_shape=(jax....]
    pallas_call x0 -> x1, Pallas kernels: none -> 4.16 us  [per_device(): pl.pallas_call(own_order, out_shape=(jax.ShapeDtypeStruct((count, members...]
    unnamed x4 -> x0, local copies, waits for them, and re-layouts: 2.72 us -> none
    slice x1 -> x0, local copies, waits for them, and re-layouts: 1.35 us -> none  [per_device(): return (new_depth, new_flow, mean[0])]
where the time goes in v1:
time: 54.5 us; the launch traced here: 54.4 us
  Pallas kernels  53.7 us (99%)
  between operations  0.64 us (1%)
    pallas_call x1, Pallas kernels, per_device(): pl.pallas_call(functools.partial(kernel, n_basin, n_ens), out_shape=(jax....  49.6 us
    pallas_call x1, Pallas kernels, per_device(): pl.pallas_call(own_order, out_shape=(jax.ShapeDtypeStruct((count, members...  4.16 us

profile of v1, /device:TPU:0, one launch (start us, length us, event | category | flops | bytes accessed | tf_op | source)
XLA Modules:
  0.0 54.4 jit_solution(3458670244751725847)
XLA Ops:
  0.6 49.6 %shard_map.103 = (f32[1024,128]{1,0:T(8,128)}, f32[1024,128]{1,0:T(8,128)}, f32[8,1024]{1,0:T(8,128)}, f32[8,128]{1,0:T(8,128)}) custom-call(s32[8,128]{1,0:T(8,128)} %bitcast.6, f32[8,128]{1,0:T(8,128)} %bitcast.7, f32[8,128]{1,0:T(8,128)} %bitcast.8, f32[8,128]{1,0:T(8,128)} %bitcast.9, f32[8,128]{1,0:T(8,128)} %bitcast.10, f32[1024,128]{1,0:T(8,128)} %depth_ref.1, ...), custom_call_target="tpu_custom_call" | custom-call | tf_op jit(solution)/shard_map/pallas_call | solution.py:435
  50.2 4.2 %shard_map.104 = (f32[1024,128]{1,0:T(8,128)}, f32[1024,128]{1,0:T(8,128)}, f32[8,128]{1,0:T(8,128)}) custom-call(f32[1024,128]{1,0:T(8,128)} %get-tuple-element.10.depth_ref, f32[1024,128]{1,0:T(8,128)} %get-tuple-element.11.flow_ref, f32[8,1024]{1,0:T(8,128)} %get-tuple-element.12.mean_ref, f32[8,128]{1,0:T(8,128)} %get-tuple-element.13.place_ref), custom_call_target="tpu_custom_call" | custom-call | tf_op jit(solution)/shard_map/pallas_call | solution.py:476
